TPU v7x, 32 devices: a whole 2x2x4 slice. The times are simulated.
32 devices in a mesh: replica: 4 (over y, core), tensor: 8 (over z, x).
Axes of the slice: x: 2, y: 2, z: 4, core: 2. Of those that a mesh axis runs over, the one named last changes fastest.
Arguments:
- tokens: bfloat16 [4, 2048, 8192], P('replica', None, 'tensor'), may hold values from -6 to 6
- kv_grad: bfloat16 [4, 2048, 1024], P('replica', None, 'tensor'), may hold values from -6 to 6
- weights: float32 [4, 8192, 1024], P('replica', 'tensor'), may hold values from -0.0625 to 0.0625
- first_moment: bfloat16 [4, 8192, 1024], P('replica', 'tensor'), may hold values from -240 to 240
- second_moment: bfloat16 [4, 8192, 1024], P('replica', 'tensor'), may hold values from 300 to 5984
- exponent: int32 [8], replicated, may hold values from 0 to 1, as said below
Outputs:
- new_weights: float32 [4, 8192, 1024], P('replica', 'tensor')
- new_first: bfloat16 [4, 8192, 1024], P('replica', 'tensor')
- new_second: bfloat16 [4, 8192, 1024], P('replica', 'tensor')
- input_grad: bfloat16 [4, 2048, 8192], P('replica', None, 'tensor')
Inputs may be any that keep to these rules, and one draw needn't show every extreme that they name: One integer per column bucket; the gossip partner of bucket g lies 2 ** exponent[g] replicas away; some bucket takes 0 and some bucket takes the largest allowed value.
All inputs are finite; a program needn't handle non-finite values.
Results may differ from a plain program's by a relative error of at most 0.0049.
Values may be sent and summed in bfloat16 or wider, within the bound.
A program may use at most 128 MiB of HBM per device.

v0:
```python
import jax
import jax.numpy as jnp
from jax import lax
from jax.sharding import PartitionSpec as P

learn_rate = 0.00015
beta_first = 0.9
beta_second = 0.95
decay_rate = 0.1
epsilon = 1e-08


def for_sending(array):
    return jax.tree.map(lambda a: a.astype(jnp.bfloat16) if a.dtype == jnp.float32 else a, array)


def from_behind(array, axis, by):
    count = lax.axis_size(axis)
    return lax.ppermute(array, axis, [(i, (i + by) % count) for i in range(count)])


def build_branch(hop_count):

    def fetch_peer(source_array):
        return jax.tree.map(
            lambda part, own: part.astype(own.dtype),
            from_behind(for_sending(source_array), "replica", hop_count),
            source_array,
        )

    return fetch_peer


def bucket_gossip(source_array, exponent, builder):
    levels = lax.axis_size("replica").bit_length() - 1
    branches = [builder(1 << bit_index) for bit_index in range(levels)]
    bucket_count = exponent.shape[0]
    bucket_width = source_array.shape[2] // bucket_count
    pieces = []
    for bucket_index in range(bucket_count):
        columns = source_array[
            :, :, bucket_index * bucket_width : (bucket_index + 1) * bucket_width
        ]
        pieces.append(lax.switch(exponent[bucket_index], branches, columns))
    return jnp.concatenate(pieces, axis=2)


def adam_update(master_part, partner_part, grad_part, first_part, second_part):
    averaged = 0.5 * (master_part + partner_part)
    first = beta_first * first_part.astype(jnp.float32) + (1.0 - beta_first) * grad_part
    second = (
        beta_second * second_part.astype(jnp.float32) + (1.0 - beta_second) * grad_part * grad_part
    )
    direction = first / (jnp.sqrt(second) + epsilon)
    new_weights = averaged - learn_rate * (direction + decay_rate * averaged)
    return (new_weights, first.astype(jnp.bfloat16), second.astype(jnp.bfloat16))


def on_device(tokens, kv_grad, weights, first_moment, second_moment, exponent):
    acts = tokens[0]
    local_cols = kv_grad[0]
    master = weights[0]
    master_low = master.astype(jnp.bfloat16)
    whole_grad = lax.all_gather(local_cols, "tensor", axis=1, tiled=True)
    grad_here = jnp.dot(acts.T, whole_grad, preferred_element_type=jnp.float32)
    back = jnp.dot(whole_grad, master_low.T, preferred_element_type=jnp.float32)
    partner = bucket_gossip(weights, exponent, build_branch)
    new_weights, new_first, new_second = adam_update(
        master, partner[0], grad_here, first_moment[0], second_moment[0]
    )
    return (new_weights[None], new_first[None], new_second[None], back.astype(jnp.bfloat16)[None])


def solution(mesh):
    placed = (
        P("replica", None, "tensor"),
        P("replica", None, "tensor"),
        P("replica", "tensor", None),
        P("replica", "tensor", None),
        P("replica", "tensor", None),
        P(),
    )
    return jax.shard_map(
        on_device,
        mesh=mesh,
        in_specs=placed,
        out_specs=(
            P("replica", "tensor", None),
            P("replica", "tensor", None),
            P("replica", "tensor", None),
            P("replica", None, "tensor"),
        ),
        check_vma=False,
    )
```

profile of v0, /device:TPU:0, one launch (start us, length us, event | category | flops | bytes accessed | tf_op | source)
XLA Modules:
  0.0 116.2 jit_solution(7453863151235359083)
XLA Ops:
  7.9 1.6 %fusion.18 = (s32[1]{0:T(128)}, s32[1]{0:T(128)}, s32[1]{0:T(128)}, s32[1]{0:T(128)}, s32[1]{0:T(128)}, /*index=5*/s32[1]{0:T(128)}, s32[1]{0:T(128)}, s32[1]{0:T(128)}) fusion(s32[8]{0:T(128)} %param.27), kind=kLoop, calls=%fused_computation.28 | loop fusion | bytes 64 | tf_op jit(solution)/shard_map/slice | solution.py:44
  14.8 3.2 %fusion.17 = (bf16[1,1024,128]{2,1,0:T(8,128)(2,1)S(1)}, bf16[1,1024,128]{2,1,0:T(8,128)(2,1)}, bf16[1,1024,128]{2,1,0:T(8,128)(2,1)S(1)}, bf16[1,1024,128]{2,1,...) fusion(f32[1,1024,1024]{2,1,0:T(8,128)} %param.24), kind=kLoop, calls=%fused_computation.27 | loop fusion | bytes 4194304 | tf_op jit(solution)/shard_map/slice | solution.py:41
  18.0 6.5 %conditional.32 = (f32[1,1024,128]{2,1,0:T(8,128)S(1)}) conditional(s32[]{:T(128)} %bitcast, bf16[1,1024,128]{2,1,0:T(8,128)(2,1)S(1)} %get-tuple-element.102, bf16[1,1024,128]{2,1,0:T(8,128)(2,1)S(1)} %get-tuple-element.102), branch_computations={%region_0.0_spmd, %region_1.0_spmd} | conditional | flops 131072 | bytes 1835056
  18.5 6.0 %collective-permute-done = bf16[1,1024,128]{2,1,0:T(8,128)(2,1)S(1)} collective-permute-done((bf16[1,1024,128]{2,1,0:T(8,128)(2,1)S(1)}, bf16[1,1024,128]{2,1,0:T(8,128)(2,1)S(1)}, u32[]{:S(2)}, u32[]{:S(2)}) %collective-permute-start) | collective-permute-done | bytes 262176 | tf_op jit(solution)/shard_map/cond/branch_0_fun/ppermute | solution.py:19
  24.5 5.9 %conditional.33 = (f32[1,1024,128]{2,1,0:T(8,128)S(1)}) conditional(s32[]{:T(128)} %bitcast.1, bf16[1,1024,128]{2,1,0:T(8,128)(2,1)S(1)} %get-tuple-element.101, bf16[1,1024,128]{2,1,0:T(8,128)(2,1)S(1)} %get-tuple-element.101), branch_computations={%region_2.0_spmd, %region_3.0_spmd} | conditional | flops 131072 | bytes 1835056
  24.6 5.8 %collective-permute-done.2 = bf16[1,1024,128]{2,1,0:T(8,128)(2,1)S(1)} collective-permute-done((bf16[1,1024,128]{2,1,0:T(8,128)(2,1)S(1)}, bf16[1,1024,128]{2,1,0:T(8,128)(2,1)S(1)}, u32[]{:S(2)}, u32[]{:S(2)}) %collective-permute-start.2) | collective-permute-done | bytes 262176 | tf_op jit(solution)/shard_map/cond/branch_0_fun/ppermute | solution.py:19
  30.5 5.9 %conditional.34 = (f32[1,1024,128]{2,1,0:T(8,128)S(1)}) conditional(s32[]{:T(128)} %bitcast.2, bf16[1,1024,128]{2,1,0:T(8,128)(2,1)S(1)} %get-tuple-element.100, bf16[1,1024,128]{2,1,0:T(8,128)(2,1)S(1)} %get-tuple-element.100), branch_computations={%region_4.0_spmd, %region_5.0_spmd} | conditional | flops 131072 | bytes 1835056
  30.5 5.8 %collective-permute-done.4 = bf16[1,1024,128]{2,1,0:T(8,128)(2,1)S(1)} collective-permute-done((bf16[1,1024,128]{2,1,0:T(8,128)(2,1)S(1)}, bf16[1,1024,128]{2,1,0:T(8,128)(2,1)S(1)}, u32[]{:S(2)}, u32[]{:S(2)}) %collective-permute-start.4) | collective-permute-done | bytes 262176 | tf_op jit(solution)/shard_map/cond/branch_0_fun/ppermute | solution.py:19
  36.4 8.3 %conditional.35 = (f32[1,1024,128]{2,1,0:T(8,128)S(1)}) conditional(s32[]{:T(128)} %bitcast.3, bf16[1,1024,128]{2,1,0:T(8,128)(2,1)S(1)} %get-tuple-element.99, bf16[1,1024,128]{2,1,0:T(8,128)(2,1)S(1)} %get-tuple-element.99), branch_computations={%region_6.0_spmd, %region_7.0_spmd} | conditional | flops 131072 | bytes 1835056
  36.4 2.4 %collective-permute-start.7 = (bf16[1,1024,128]{2,1,0:T(8,128)(2,1)S(1)}, bf16[1,1024,128]{2,1,0:T(8,128)(2,1)S(1)}, u32[]{:S(2)}, u32[]{:S(2)}) collective-permute-start(bf16[1,1024,128]{2,1,0:T(8,128)(2,1)S(1)} %param.7), channel_id=1, source_target_pairs={{0,16},{8,24},{16,0},{24,8},{1,17},{9,25},{17,1},{25,9},{2,18},{10... | collective-permute-start | bytes 786440 | tf_op jit(solution)/shard_map/cond/branch_1_fun/ppermute | solution.py:19
  38.8 5.8 %collective-permute-done.7 = bf16[1,1024,128]{2,1,0:T(8,128)(2,1)S(1)} collective-permute-done((bf16[1,1024,128]{2,1,0:T(8,128)(2,1)S(1)}, bf16[1,1024,128]{2,1,0:T(8,128)(2,1)S(1)}, u32[]{:S(2)}, u32[]{:S(2)}) %collective-permute-start.7) | collective-permute-done | bytes 262176 | tf_op jit(solution)/shard_map/cond/branch_1_fun/ppermute | solution.py:19
  44.6 5.9 %conditional.36 = (f32[1,1024,128]{2,1,0:T(8,128)S(1)}) conditional(s32[]{:T(128)} %bitcast.4, bf16[1,1024,128]{2,1,0:T(8,128)(2,1)S(1)} %get-tuple-element.98, bf16[1,1024,128]{2,1,0:T(8,128)(2,1)S(1)} %get-tuple-element.98), branch_computations={%region_8.0_spmd, %region_9.0_spmd} | conditional | flops 131072 | bytes 1835056
  44.7 5.8 %collective-permute-done.8 = bf16[1,1024,128]{2,1,0:T(8,128)(2,1)S(1)} collective-permute-done((bf16[1,1024,128]{2,1,0:T(8,128)(2,1)S(1)}, bf16[1,1024,128]{2,1,0:T(8,128)(2,1)S(1)}, u32[]{:S(2)}, u32[]{:S(2)}) %collective-permute-start.8) | collective-permute-done | bytes 262176 | tf_op jit(solution)/shard_map/cond/branch_0_fun/ppermute | solution.py:19
  50.6 6.5 %conditional.37 = (f32[1,1024,128]{2,1,0:T(8,128)S(1)}) conditional(s32[]{:T(128)} %bitcast.5, bf16[1,1024,128]{2,1,0:T(8,128)(2,1)S(1)} %get-tuple-element.97, bf16[1,1024,128]{2,1,0:T(8,128)(2,1)S(1)} %get-tuple-element.97), branch_computations={%region_10.0_spmd, %region_11.0_spmd} | conditional | flops 131072 | bytes 1835056
  51.2 5.8 %collective-permute-done.11 = bf16[1,1024,128]{2,1,0:T(8,128)(2,1)S(1)} collective-permute-done((bf16[1,1024,128]{2,1,0:T(8,128)(2,1)S(1)}, bf16[1,1024,128]{2,1,0:T(8,128)(2,1)S(1)}, u32[]{:S(2)}, u32[]{:S(2)}) %collective-permute-start.11) | collective-permute-done | bytes 262176 | tf_op jit(solution)/shard_map/cond/branch_1_fun/ppermute | solution.py:19
  57.1 7.5 %conditional.38 = (f32[1,1024,128]{2,1,0:T(8,128)}) conditional(s32[]{:T(128)} %bitcast.6, bf16[1,1024,128]{2,1,0:T(8,128)(2,1)} %get-tuple-element.96, bf16[1,1024,128]{2,1,0:T(8,128)(2,1)} %get-tuple-element.96), branch_computations={%region_12.0_spmd, %region_13.0_spmd} | conditional | flops 131072 | bytes 1835056
  57.1 1.6 %collective-permute-start.13 = (bf16[1,1024,128]{2,1,0:T(8,128)(2,1)}, bf16[1,1024,128]{2,1,0:T(8,128)(2,1)S(1)}, u32[]{:S(2)}, u32[]{:S(2)}) collective-permute-start(bf16[1,1024,128]{2,1,0:T(8,128)(2,1)} %param.13), channel_id=1, source_target_pairs={{0,16},{8,24},{16,0},{24,8},{1,17},{9,25},{17,1},{25,9},{2,18},{10... | collective-permute-start | bytes 786440 | tf_op jit(solution)/shard_map/cond/branch_1_fun/ppermute | solution.py:19
  58.7 5.1 %collective-permute-done.13 = bf16[1,1024,128]{2,1,0:T(8,128)(2,1)S(1)} collective-permute-done((bf16[1,1024,128]{2,1,0:T(8,128)(2,1)}, bf16[1,1024,128]{2,1,0:T(8,128)(2,1)S(1)}, u32[]{:S(2)}, u32[]{:S(2)}) %collective-permute-start.13) | collective-permute-done | bytes 262176 | tf_op jit(solution)/shard_map/cond/branch_1_fun/ppermute | solution.py:19
  63.7 0.8 convert_element_type.155
  64.6 6.6 %conditional.39 = (f32[1,1024,128]{2,1,0:T(8,128)}) conditional(s32[]{:T(128)} %bitcast.7, bf16[1,1024,128]{2,1,0:T(8,128)(2,1)S(1)} %get-tuple-element.95, bf16[1,1024,128]{2,1,0:T(8,128)(2,1)S(1)} %get-tuple-element.95), branch_computations={%region_14.0_spmd, %region_15.0_spmd} | conditional | flops 131072 | bytes 1835056
  64.6 5.8 %collective-permute-done.14 = bf16[1,1024,128]{2,1,0:T(8,128)(2,1)S(1)} collective-permute-done((bf16[1,1024,128]{2,1,0:T(8,128)(2,1)S(1)}, bf16[1,1024,128]{2,1,0:T(8,128)(2,1)S(1)}, u32[]{:S(2)}, u32[]{:S(2)}) %collective-permute-start.14) | collective-permute-done | bytes 262176 | tf_op jit(solution)/shard_map/cond/branch_0_fun/ppermute | solution.py:19
  70.4 0.8 convert_element_type.157
  71.2 0.8 constant_dynamic-update-slice_fusion.7
  72.0 0.8 constant_dynamic-update-slice_fusion.6
  72.9 0.8 constant_dynamic-update-slice_fusion.5
  73.7 0.8 constant_dynamic-update-slice_fusion.4
  74.5 0.8 constant_dynamic-update-slice_fusion.3
  76.2 0.8 constant_dynamic-update-slice_fusion.1
  77.0 0.8 constant_dynamic-update-slice_fusion
  77.8 10.0 %all-gather.3.cloned.1.call-done = bf16[1,2048,1024]{2,1,0:T(8,128)(2,1)} async-done(((bf16[1,2048,128]{2,1,0:T(8,128)(2,1)}), bf16[1,2048,1024]{2,1,0:T(8,128)(2,1)}) %all-gather.3.cloned.1.call-update) | async-done | bytes 4194320 | tf_op jit(solution)/shard_map/all_gather | solution.py:64
  87.8 10.2 %convert_bitcast_fusion = bf16[1,2048,1024]{2,1,0:T(8,128)(2,1)} fusion(bf16[1,2048,1024]{2,1,0:T(8,128)(2,1)} %all-gather.3.cloned.1.call-done, f32[1,1024,1024]{2,1,0:T(8,128)} %param.24), kind=kOutput, calls=%fused_computation.12 | convolution fusion | flops 4298113024 | bytes 12582912 | tf_op jit(solution)/shard_map/dot_general | solution.py:66
  98.0 11.3 %fusion.13 = (bf16[1,1024,1024]{2,1,0:T(8,128)(2,1)}, f32[1,1024,1024]{2,1,0:T(8,128)}, bf16[1,1024,1024]{2,1,0:T(8,128)(2,1)}) fusion(bf16[1,1024,1024]{2,1,0:T(8,128)(2,1)S(1)} %copy-done.5, bf16[1,1024,1024]{2,1,0:T(8,128)(2,1)S(1)} %copy-done.6, f32[1,1024,1024]{2,1,0:T(8,128)S(1)} %copy-done.2, f32[1,1024,1024]{2,1,0:T(8,128)} %constant_dynamic-update-slice_fusion, ...), kind=kOutput, calls=%fused_computation.15 | convolution fusion | flops 4314890240 | bytes 29360128 | tf_op jit(solution)/shard_map/dot_general | solution.py:65
  (29 shorter events, 3.0 us)
Async XLA Ops:
  7.2 80.6 %all-gather.3.cloned.1.call-start = ((), (), s32[]{:S(2)}) async-start(), calls=%async_computation | async-start | bytes 4718592 | tf_op jit(solution)/shard_map/all_gather | solution.py:64
  18.0 6.5 %collective-permute-start = (bf16[1,1024,128]{2,1,0:T(8,128)(2,1)S(1)}, bf16[1,1024,128]{2,1,0:T(8,128)(2,1)S(1)}, u32[]{:S(2)}, u32[]{:S(2)}) collective-permute-start(bf16[1,1024,128]{2,1,0:T(8,128)(2,1)S(1)} %param), channel_id=1, source_target_pairs={{0,8},{8,16},{16,24},{24,0},{1,9},{9,17},{17,25},{25,1},{2,10},{10... | collective-permute-start | bytes 786440 | tf_op jit(solution)/shard_map/cond/branch_0_fun/ppermute | solution.py:19
  24.6 5.8 %collective-permute-start.2 = (bf16[1,1024,128]{2,1,0:T(8,128)(2,1)S(1)}, bf16[1,1024,128]{2,1,0:T(8,128)(2,1)S(1)}, u32[]{:S(2)}, u32[]{:S(2)}) collective-permute-start(bf16[1,1024,128]{2,1,0:T(8,128)(2,1)S(1)} %param.2), channel_id=1, source_target_pairs={{0,8},{8,16},{16,24},{24,0},{1,9},{9,17},{17,25},{25,1},{2,10},{10... | collective-permute-start | bytes 786440 | tf_op jit(solution)/shard_map/cond/branch_0_fun/ppermute | solution.py:19
  30.5 5.8 %collective-permute-start.4 = (bf16[1,1024,128]{2,1,0:T(8,128)(2,1)S(1)}, bf16[1,1024,128]{2,1,0:T(8,128)(2,1)S(1)}, u32[]{:S(2)}, u32[]{:S(2)}) collective-permute-start(bf16[1,1024,128]{2,1,0:T(8,128)(2,1)S(1)} %param.4), channel_id=1, source_target_pairs={{0,8},{8,16},{16,24},{24,0},{1,9},{9,17},{17,25},{25,1},{2,10},{10... | collective-permute-start | bytes 786440 | tf_op jit(solution)/shard_map/cond/branch_0_fun/ppermute | solution.py:19
  36.4 8.2 %collective-permute-start.7 = (bf16[1,1024,128]{2,1,0:T(8,128)(2,1)S(1)}, bf16[1,1024,128]{2,1,0:T(8,128)(2,1)S(1)}, u32[]{:S(2)}, u32[]{:S(2)}) collective-permute-start(bf16[1,1024,128]{2,1,0:T(8,128)(2,1)S(1)} %param.7), channel_id=1, source_target_pairs={{0,16},{8,24},{16,0},{24,8},{1,17},{9,25},{17,1},{25,9},{2,18},{10... | collective-permute-start | bytes 786440 | tf_op jit(solution)/shard_map/cond/branch_1_fun/ppermute | solution.py:19
  44.7 5.8 %collective-permute-start.8 = (bf16[1,1024,128]{2,1,0:T(8,128)(2,1)S(1)}, bf16[1,1024,128]{2,1,0:T(8,128)(2,1)S(1)}, u32[]{:S(2)}, u32[]{:S(2)}) collective-permute-start(bf16[1,1024,128]{2,1,0:T(8,128)(2,1)S(1)} %param.8), channel_id=1, source_target_pairs={{0,8},{8,16},{16,24},{24,0},{1,9},{9,17},{17,25},{25,1},{2,10},{10... | collective-permute-start | bytes 786440 | tf_op jit(solution)/shard_map/cond/branch_0_fun/ppermute | solution.py:19
  50.6 6.4 %collective-permute-start.11 = (bf16[1,1024,128]{2,1,0:T(8,128)(2,1)S(1)}, bf16[1,1024,128]{2,1,0:T(8,128)(2,1)S(1)}, u32[]{:S(2)}, u32[]{:S(2)}) collective-permute-start(bf16[1,1024,128]{2,1,0:T(8,128)(2,1)S(1)} %param.11), channel_id=1, source_target_pairs={{0,16},{8,24},{16,0},{24,8},{1,17},{9,25},{17,1},{25,9},{2,18},{10... | collective-permute-start | bytes 786440 | tf_op jit(solution)/shard_map/cond/branch_1_fun/ppermute | solution.py:19
  57.1 6.6 %collective-permute-start.13 = (bf16[1,1024,128]{2,1,0:T(8,128)(2,1)}, bf16[1,1024,128]{2,1,0:T(8,128)(2,1)S(1)}, u32[]{:S(2)}, u32[]{:S(2)}) collective-permute-start(bf16[1,1024,128]{2,1,0:T(8,128)(2,1)} %param.13), channel_id=1, source_target_pairs={{0,16},{8,24},{16,0},{24,8},{1,17},{9,25},{17,1},{25,9},{2,18},{10... | collective-permute-start | bytes 786440 | tf_op jit(solution)/shard_map/cond/branch_1_fun/ppermute | solution.py:19
  64.6 5.8 %collective-permute-start.14 = (bf16[1,1024,128]{2,1,0:T(8,128)(2,1)S(1)}, bf16[1,1024,128]{2,1,0:T(8,128)(2,1)S(1)}, u32[]{:S(2)}, u32[]{:S(2)}) collective-permute-start(bf16[1,1024,128]{2,1,0:T(8,128)(2,1)S(1)} %param.14), channel_id=1, source_target_pairs={{0,8},{8,16},{16,24},{24,0},{1,9},{9,17},{17,25},{25,1},{2,10},{10... | collective-permute-start | bytes 786440 | tf_op jit(solution)/shard_map/cond/branch_0_fun/ppermute | solution.py:19
  71.2 5.0 %copy-start = (f32[1,1024,128]{2,1,0:T(8,128)S(1)}, f32[1,1024,128]{2,1,0:T(8,128)}, u32[]{:S(2)}) copy-start(f32[1,1024,128]{2,1,0:T(8,128)} %get-tuple-element.117) | copy-start | bytes 1572868
  71.2 5.8 %copy-start.1 = (f32[1,1024,128]{2,1,0:T(8,128)S(1)}, f32[1,1024,128]{2,1,0:T(8,128)}, u32[]{:S(2)}) copy-start(f32[1,1024,128]{2,1,0:T(8,128)} %get-tuple-element.118) | copy-start | bytes 1572868
  87.8 10.2 %copy-start.2 = (f32[1,1024,1024]{2,1,0:T(8,128)S(1)}, f32[1,1024,1024]{2,1,0:T(8,128)}, u32[]{:S(2)}) copy-start(f32[1,1024,1024]{2,1,0:T(8,128)} %param.24) | copy-start | bytes 12582916
  87.8 10.2 %copy-start.3 = (bf16[1,2048,1024]{2,1,0:T(8,128)(2,1)S(1)}, bf16[1,2048,1024]{2,1,0:T(8,128)(2,1)}, u32[]{:S(2)}) copy-start(bf16[1,2048,1024]{2,1,0:T(8,128)(2,1)} %param.22) | copy-start | bytes 12582916
  87.8 10.2 %copy-start.4 = (bf16[1,2048,1024]{2,1,0:T(8,128)(2,1)S(1)}, bf16[1,2048,1024]{2,1,0:T(8,128)(2,1)}, u32[]{:S(2)}) copy-start(bf16[1,2048,1024]{2,1,0:T(8,128)(2,1)} %all-gather.3.cloned.1.call-done) | copy-start | bytes 12582916
  87.8 10.2 %copy-start.5 = (bf16[1,1024,1024]{2,1,0:T(8,128)(2,1)S(1)}, bf16[1,1024,1024]{2,1,0:T(8,128)(2,1)}, u32[]{:S(2)}) copy-start(bf16[1,1024,1024]{2,1,0:T(8,128)(2,1)} %param.26) | copy-start | bytes 6291460
  87.8 10.2 %copy-start.6 = (bf16[1,1024,1024]{2,1,0:T(8,128)(2,1)S(1)}, bf16[1,1024,1024]{2,1,0:T(8,128)(2,1)}, u32[]{:S(2)}) copy-start(bf16[1,1024,1024]{2,1,0:T(8,128)(2,1)} %param.25) | copy-start | bytes 6291460
Sparse Core Ops, SparseCore 0:
  10.0 77.7 all-gather.2
where the time goes:
time: 116 us
  waiting for transfers between devices  56.6 us (49%)
  matrix products  21.5 us (19%)
  between operations  19.4 us (17%)
  local copies, waits for them, and re-layouts  11.5 us (10%)
  starting transfers between devices  5.19 us (4%)
  other arithmetic  1.87 us (2%)
    ppermute x8, waiting for transfers between devices, from_behind(): lax.ppermute(array, axis, [(i, (i + by) % count) for i in range(count)])  45.9 us
    dot_general x1, matrix products, on_device(): grad_here = jnp.dot(acts.T, whole_grad, preferred_element_type=jnp.float32)  11.3 us
    dot_general x1, matrix products, on_device(): back = jnp.dot(whole_grad, master_low.T, preferred_element_type=jnp.float32)  10.2 us
    all_gather x1, waiting for transfers between devices, on_device(): whole_grad = lax.all_gather(local_cols, 'tensor', axis=1, tiled=True)  9.97 us
    unnamed x21, local copies, waits for them, and re-layouts  5.81 us
    ppermute x8, starting transfers between devices, from_behind(): lax.ppermute(array, axis, [(i, (i + by) % count) for i in range(count)])  5.15 us
    slice x1, local copies, waits for them, and re-layouts, bucket_gossip(): source_array[:, :, bucket_index * bucket_width:(bucket_index + 1) * bucke...  3.25 us
  transfers between devices with their start and end apart: 9, of which 9 were waited for; matrix products, arithmetic and copies ran while one was open for 12% of the time, Pallas kernels for 0%

commit v1 on v0

--- a/solution.py
+++ b/solution.py
@@ -61,7 +61,29 @@
     local_cols = kv_grad[0]
     master = weights[0]
     master_low = master.astype(jnp.bfloat16)
-    whole_grad = lax.all_gather(local_cols, "tensor", axis=1, tiled=True)
+    shares = lax.axis_size("tensor")
+    bank = []
+    i0 = 0
+    while i0 < shares:
+        bank.append((i0, (i0 + 1) % shares))
+        i0 += 1
+    rows = []
+    i0 = 0
+    while i0 < shares:
+        rows.append((i0, (i0 - 1) % shares))
+        i0 += 1
+    y1, latest = ([local_cols], [local_cols])
+    for _ in range(shares // 2):
+        tile_out = lax.ppermute(y1[-1], "tensor", bank)
+        y1.append(tile_out)
+    dev_j = 0
+    while dev_j < (shares - 1) // 2:
+        val = lax.ppermute(latest[-1], "tensor", rows)
+        latest.append(val)
+        dev_j += 1
+    reached = jnp.concatenate([*y1[::-1], *latest[1:]], axis=1)
+    reply = lax.axis_index("tensor")
+    whole_grad = jnp.roll(reached, (reply - shares // 2) * local_cols.shape[1], axis=1)
     grad_here = jnp.dot(acts.T, whole_grad, preferred_element_type=jnp.float32)
     back = jnp.dot(whole_grad, master_low.T, preferred_element_type=jnp.float32)
     partner = bucket_gossip(weights, exponent, build_branch)

time: 116 us -> 188 us (1.62)
  local copies, waits for them, and re-layouts: 11.5 us -> 61 us
  waiting for transfers between devices: 56.6 us -> 81.7 us
  starting transfers between devices: 5.19 us -> 20.7 us
  between operations: 19.4 us -> 5.95 us
  matrix products: 21.5 us -> 17.7 us
    unnamed x21 -> x46, local copies, waits for them, and re-layouts: 5.81 us -> 42.2 us
    ppermute x0 -> x7, waiting for transfers between devices: none -> 34.5 us  [the longest x4 28.4 us: on_device(): tile_out = lax.ppermute(y1[-1], 'tensor', bank)]
    ppermute x0 -> x7, starting transfers between devices: none -> 17.2 us  [the longest x3 11.7 us: on_device(): val = lax.ppermute(latest[-1], 'tensor', rows)]
    another operation x0 -> x8, local copies, waits for them, and re-layouts: none -> 11.7 us
    all_gather x1 -> x0, waiting for transfers between devices: 9.97 us -> none  [on_device(): whole_grad = lax.all_gather(local_cols, 'tensor', axis=1, tiled=True)]
    dot_general x1, matrix products: 10.2 us -> 6.28 us  [on_device(): back = jnp.dot(whole_grad, master_low.T, preferred_element_type=jnp.float32)]
  transfers between devices with their start and end apart: 9 -> 15, of which waited for: 9 -> 11; matrix products, arithmetic and copies ran while one was open for 12% -> 24% of each run, Pallas kernels for 0% -> 0%
where the time goes in v1:
time: 188 us; the launch traced here: 187 us
  waiting for transfers between devices  81.7 us (43%)
  local copies, waits for them, and re-layouts  61 us (32%)
  starting transfers between devices  20.7 us (11%)
  matrix products  17.7 us (9%)
  between operations  5.95 us (3%)
    ppermute x8, waiting for transfers between devices, from_behind(): lax.ppermute(array, axis, [(i, (i + by) % count) for i in range(count)])  47.2 us
    unnamed x46, local copies, waits for them, and re-layouts  42.2 us
    ppermute x4, waiting for transfers between devices, on_device(): tile_out = lax.ppermute(y1[-1], 'tensor', bank)  28.4 us
    another operation x8, local copies, waits for them, and re-layouts  11.7 us
    ppermute x3, starting transfers between devices, on_device(): val = lax.ppermute(latest[-1], 'tensor', rows)  11.7 us
    dot_general x1, matrix products, on_device(): grad_here = jnp.dot(acts.T, whole_grad, preferred_element_type=jnp.float32)  11.4 us
    dot_general x1, matrix products, on_device(): back = jnp.dot(whole_grad, master_low.T, preferred_element_type=jnp.float32)  6.28 us
    ppermute x3, waiting for transfers between devices, on_device(): val = lax.ppermute(latest[-1], 'tensor', rows)  6.09 us
  transfers between devices with their start and end apart: 15, of which 11 were waited for; matrix products, arithmetic and copies ran while one was open for 24% of the time, Pallas kernels for 0%

profile of v1, /device:TPU:0, one launch (start us, length us, event | category | flops | bytes accessed | tf_op | source)
XLA Modules:
  0.0 187.2 jit_solution(9642823332393618683)
XLA Ops:
  0.6 3.0 %collective-permute-start.16 = (bf16[2048,128]{1,0:T(8,128)(2,1)}, bf16[2048,128]{1,0:T(8,128)(2,1)S(1)}, u32[]{:S(2)}, u32[]{:S(2)}) collective-permute-start(bf16[2048,128]{1,0:T(8,128)(2,1)} %bitcast.70), channel_id=1, source_target_pairs={{0,1},{1,2},{2,3},{3,4},{4,5},{5,6},{6,7},{7,0},{8,9},{9,10},{10,1... | collective-permute-start | bytes 1572872 | tf_op jit(solution)/shard_map/ppermute | solution.py:77
  3.6 15.2 %collective-permute-done.16 = bf16[2048,128]{1,0:T(8,128)(2,1)S(1)} collective-permute-done((bf16[2048,128]{1,0:T(8,128)(2,1)}, bf16[2048,128]{1,0:T(8,128)(2,1)S(1)}, u32[]{:S(2)}, u32[]{:S(2)}) %collective-permute-start.16) | collective-permute-done | bytes 524320 | tf_op jit(solution)/shard_map/ppermute | solution.py:77
  18.8 4.7 %collective-permute-start.20 = (bf16[2048,128]{1,0:T(8,128)(2,1)}, bf16[2048,128]{1,0:T(8,128)(2,1)S(1)}, u32[]{:S(2)}, u32[]{:S(2)}) collective-permute-start(bf16[2048,128]{1,0:T(8,128)(2,1)} %bitcast.71), channel_id=1, source_target_pairs={{0,7},{1,0},{2,1},{3,2},{4,3},{5,4},{6,5},{7,6},{8,15},{9,8},{10,9... | collective-permute-start | bytes 1572872 | tf_op jit(solution)/shard_map/ppermute | solution.py:81
  27.7 13.2 %collective-permute-done.17 = bf16[2048,128]{1,0:T(8,128)(2,1)S(1)} collective-permute-done((bf16[2048,128]{1,0:T(8,128)(2,1)S(1)}, bf16[2048,128]{1,0:T(8,128)(2,1)S(1)}, u32[]{:S(2)}, u32[]{:S(2)}) %collective-permute-start.17) | collective-permute-done | bytes 524320 | tf_op jit(solution)/shard_map/ppermute | solution.py:77
  40.9 2.5 %collective-permute-start.18 = (bf16[2048,128]{1,0:T(8,128)(2,1)S(1)}, bf16[2048,128]{1,0:T(8,128)(2,1)}, u32[]{:S(2)}, u32[]{:S(2)}) collective-permute-start(bf16[2048,128]{1,0:T(8,128)(2,1)S(1)} %collective-permute-done.17), channel_id=1, source_target_pairs={{0,1},{1,2},{2,3},{3,4},{4,5},{5,6},{6,7},{7,0},{8,9},{9,10},{10,1... | collective-permute-start | bytes 1572872 | tf_op jit(solution)/shard_map/ppermute | solution.py:77
  43.4 3.4 %fusion.17 = (bf16[1,1024,128]{2,1,0:T(8,128)(2,1)S(1)}, bf16[1,1024,128]{2,1,0:T(8,128)(2,1)}, bf16[1,1024,128]{2,1,0:T(8,128)(2,1)}, bf16[1,1024,128]{2,1,0:T(...) fusion(f32[1,1024,1024]{2,1,0:T(8,128)} %param.24), kind=kLoop, calls=%fused_computation.45 | loop fusion | bytes 4194304 | tf_op jit(solution)/shard_map/slice | solution.py:41
  46.8 5.9 %conditional.32 = (f32[1,1024,128]{1,2,0:T(8,128)S(1)}) conditional(s32[]{:T(128)} %bitcast, bf16[1,1024,128]{2,1,0:T(8,128)(2,1)S(1)} %get-tuple-element.114, bf16[1,1024,128]{2,1,0:T(8,128)(2,1)S(1)} %get-tuple-element.114), branch_computations={%region_0.1_spmd, %region_1.2_spmd} | conditional | bytes 1835056
  46.8 5.8 %collective-permute-done = bf16[1,1024,128]{2,1,0:T(8,128)(2,1)S(1)} collective-permute-done((bf16[1,1024,128]{2,1,0:T(8,128)(2,1)S(1)}, bf16[1,1024,128]{2,1,0:T(8,128)(2,1)S(1)}, u32[]{:S(2)}, u32[]{:S(2)}) %collective-permute-start) | collective-permute-done | bytes 262176 | tf_op jit(solution)/shard_map/cond/branch_0_fun/ppermute | solution.py:19
  52.7 7.1 %conditional.33 = (f32[1,1024,128]{1,2,0:T(8,128)S(1)}) conditional(s32[]{:T(128)} %bitcast.1, bf16[1,1024,128]{2,1,0:T(8,128)(2,1)S(1)} %get-tuple-element.113, bf16[1,1024,128]{2,1,0:T(8,128)(2,1)S(1)} %get-tuple-element.113), branch_computations={%region_2.3_spmd, %region_3.4_spmd} | conditional | bytes 1835056
  52.8 5.9 %collective-permute-done.2 = bf16[1,1024,128]{2,1,0:T(8,128)(2,1)} collective-permute-done((bf16[1,1024,128]{2,1,0:T(8,128)(2,1)S(1)}, bf16[1,1024,128]{2,1,0:T(8,128)(2,1)}, u32[]{:S(2)}, u32[]{:S(2)}) %collective-permute-start.2) | collective-permute-done | bytes 262176 | tf_op jit(solution)/shard_map/cond/branch_0_fun/ppermute | solution.py:19
  59.8 7.1 %conditional.34 = (f32[1,1024,128]{1,2,0:T(8,128)S(1)}) conditional(s32[]{:T(128)} %bitcast.2, bf16[1,1024,128]{2,1,0:T(8,128)(2,1)S(1)} %get-tuple-element.112, bf16[1,1024,128]{2,1,0:T(8,128)(2,1)S(1)} %get-tuple-element.112), branch_computations={%region_4.5_spmd, %region_5.6_spmd} | conditional | bytes 1835056
  59.9 5.9 %collective-permute-done.4 = bf16[1,1024,128]{2,1,0:T(8,128)(2,1)} collective-permute-done((bf16[1,1024,128]{2,1,0:T(8,128)(2,1)S(1)}, bf16[1,1024,128]{2,1,0:T(8,128)(2,1)}, u32[]{:S(2)}, u32[]{:S(2)}) %collective-permute-start.4) | collective-permute-done | bytes 262176 | tf_op jit(solution)/shard_map/cond/branch_0_fun/ppermute | solution.py:19
  66.9 9.3 %conditional.35 = (f32[1,1024,128]{1,2,0:T(8,128)}) conditional(s32[]{:T(128)} %bitcast.3, bf16[1,1024,128]{2,1,0:T(8,128)(2,1)} %get-tuple-element.111, bf16[1,1024,128]{2,1,0:T(8,128)(2,1)} %get-tuple-element.111), branch_computations={%region_6.7_spmd, %region_7.8_spmd} | conditional | bytes 1835056
  68.3 6.1 %collective-permute-done.7 = bf16[1,1024,128]{2,1,0:T(8,128)(2,1)} collective-permute-done((bf16[1,1024,128]{2,1,0:T(8,128)(2,1)}, bf16[1,1024,128]{2,1,0:T(8,128)(2,1)}, u32[]{:S(2)}, u32[]{:S(2)}) %collective-permute-start.7) | collective-permute-done | bytes 262176 | tf_op jit(solution)/shard_map/cond/branch_1_fun/ppermute | solution.py:19
  82.9 5.5 %copy.18 = f32[1,1024,1024]{1,2,0:T(8,128)} copy(f32[1,1024,1024]{2,1,0:T(8,128)} %param.24) | data formatting | bytes 8388608 | tf_op args[2]
  90.9 2.6 %copy.19 = bf16[1,1024,1024]{1,2,0:T(8,128)(2,1)} copy(bf16[1,1024,1024]{2,1,0:T(8,128)(2,1)S(1)} %copy-done.2) | data formatting | bytes 4194304 | tf_op args[3]
  93.4 2.9 %copy.20 = bf16[1,1024,1024]{1,2,0:T(8,128)(2,1)S(1)} copy(bf16[1,1024,1024]{2,1,0:T(8,128)(2,1)} %param.26) | data formatting | bytes 4194304 | tf_op args[4]
  96.3 8.1 %conditional.36 = (f32[1,1024,128]{1,2,0:T(8,128)}) conditional(s32[]{:T(128)} %bitcast.4, bf16[1,1024,128]{2,1,0:T(8,128)(2,1)} %get-tuple-element.110, bf16[1,1024,128]{2,1,0:T(8,128)(2,1)} %get-tuple-element.110), branch_computations={%region_8.9_spmd, %region_9.10_spmd} | conditional | bytes 1835056
  96.4 6.1 %collective-permute-done.8 = bf16[1,1024,128]{2,1,0:T(8,128)(2,1)} collective-permute-done((bf16[1,1024,128]{2,1,0:T(8,128)(2,1)}, bf16[1,1024,128]{2,1,0:T(8,128)(2,1)}, u32[]{:S(2)}, u32[]{:S(2)}) %collective-permute-start.8) | collective-permute-done | bytes 262176 | tf_op jit(solution)/shard_map/cond/branch_0_fun/ppermute | solution.py:19
  104.4 8.8 %conditional.37 = (f32[1,1024,128]{1,2,0:T(8,128)}) conditional(s32[]{:T(128)} %bitcast.5, bf16[1,1024,128]{2,1,0:T(8,128)(2,1)} %get-tuple-element.109, bf16[1,1024,128]{2,1,0:T(8,128)(2,1)} %get-tuple-element.109), branch_computations={%region_10.11_spmd, %region_11.12_spmd} | conditional | bytes 1835056
  105.1 6.2 %collective-permute-done.11 = bf16[1,1024,128]{2,1,0:T(8,128)(2,1)} collective-permute-done((bf16[1,1024,128]{2,1,0:T(8,128)(2,1)}, bf16[1,1024,128]{2,1,0:T(8,128)(2,1)}, u32[]{:S(2)}, u32[]{:S(2)}) %collective-permute-start.11) | collective-permute-done | bytes 262176 | tf_op jit(solution)/shard_map/cond/branch_1_fun/ppermute | solution.py:19
  113.1 8.6 %conditional.38 = (f32[1,1024,128]{1,2,0:T(8,128)}) conditional(s32[]{:T(128)} %bitcast.6, bf16[1,1024,128]{2,1,0:T(8,128)(2,1)} %get-tuple-element.108, bf16[1,1024,128]{2,1,0:T(8,128)(2,1)} %get-tuple-element.108), branch_computations={%region_12.13_spmd, %region_13.14_spmd} | conditional | bytes 1835056
  114.4 5.4 %collective-permute-done.13 = bf16[1,1024,128]{2,1,0:T(8,128)(2,1)} collective-permute-done((bf16[1,1024,128]{2,1,0:T(8,128)(2,1)}, bf16[1,1024,128]{2,1,0:T(8,128)(2,1)}, u32[]{:S(2)}, u32[]{:S(2)}) %collective-permute-start.13) | collective-permute-done | bytes 262176 | tf_op jit(solution)/shard_map/cond/branch_1_fun/ppermute | solution.py:19
  121.7 7.8 %conditional.39 = (f32[1,1024,128]{1,2,0:T(8,128)}) conditional(s32[]{:T(128)} %bitcast.7, bf16[1,1024,128]{2,1,0:T(8,128)(2,1)S(1)} %get-tuple-element.107, bf16[1,1024,128]{2,1,0:T(8,128)(2,1)S(1)} %get-tuple-element.107), branch_computations={%region_14.15_spmd, %region_15.16_spmd} | conditional | bytes 1835056
  121.7 5.9 %collective-permute-done.14 = bf16[1,1024,128]{2,1,0:T(8,128)(2,1)} collective-permute-done((bf16[1,1024,128]{2,1,0:T(8,128)(2,1)S(1)}, bf16[1,1024,128]{2,1,0:T(8,128)(2,1)}, u32[]{:S(2)}, u32[]{:S(2)}) %collective-permute-start.14) | collective-permute-done | bytes 262176 | tf_op jit(solution)/shard_map/cond/branch_0_fun/ppermute | solution.py:19
  137.3 4.7 %collective-permute-start.22 = (bf16[2048,128]{1,0:T(8,128)(2,1)}, bf16[2048,128]{1,0:T(8,128)(2,1)S(1)}, u32[]{:S(2)}, u32[]{:S(2)}) collective-permute-start(bf16[2048,128]{1,0:T(8,128)(2,1)} %collective-permute-done.21), channel_id=1, source_target_pairs={{0,7},{1,0},{2,1},{3,2},{4,3},{5,4},{6,5},{7,6},{8,15},{9,8},{10,9... | collective-permute-start | bytes 1572872 | tf_op jit(solution)/shard_map/ppermute | solution.py:81
  146.4 6.1 %collective-permute-done.22 = bf16[2048,128]{1,0:T(8,128)(2,1)S(1)} collective-permute-done((bf16[2048,128]{1,0:T(8,128)(2,1)}, bf16[2048,128]{1,0:T(8,128)(2,1)S(1)}, u32[]{:S(2)}, u32[]{:S(2)}) %collective-permute-start.22) | collective-permute-done | bytes 524320 | tf_op jit(solution)/shard_map/ppermute | solution.py:81
  157.5 6.3 %convert_bitcast_fusion = bf16[1,2048,1024]{2,1,0:T(8,128)(2,1)} fusion(bf16[2048,2048]{1,0:T(8,128)(2,1)S(1)} %constant_dynamic-update-slice_fusion.8, s32[]{:T(128)S(6)} %select_n.14, f32[1,1024,1024]{2,1,0:T(8,128)S(1)} %copy-done), kind=kOutput, calls=%fused_computation.10 | convolution fusion | flops 4298113024 | bytes 12582916 | tf_op jit(solution)/shard_map/dot_general | solution.py:88
  163.8 11.4 %fusion.11 = (bf16[1,1024,1024]{1,2,0:T(8,128)(2,1)}, f32[1,1024,1024]{1,2,0:T(8,128)}, bf16[1,1024,1024]{1,2,0:T(8,128)(2,1)}) fusion(bf16[1,1024,1024]{1,2,0:T(8,128)(2,1)S(1)} %copy.20, bf16[1,1024,1024]{1,2,0:T(8,128)(2,1)S(1)} %copy-done.3, f32[1,1024,1024]{1,2,0:T(8,128)S(1)} %copy-done.1, f32[1,1024,1024]{1,2,0:T(8,128)} %constant_dynamic-update-slice_fusion, ...), kind=kOutput, calls=%fused_computation.15 | convolution fusion | flops 4314890240 | bytes 29360132 | tf_op jit(solution)/shard_map/dot_general | solution.py:87
  175.2 5.3 %copy.21 = f32[1,1024,1024]{2,1,0:T(8,128)} copy(f32[1,1024,1024]{1,2,0:T(8,128)} %get-tuple-element.105) | data formatting | bytes 8388608
  180.6 4.1 %copy.22 = bf16[1,1024,1024]{2,1,0:T(8,128)(2,1)} copy(bf16[1,1024,1024]{1,2,0:T(8,128)(2,1)} %get-tuple-element.106) | data formatting | bytes 4194304
  184.7 2.5 %copy.23 = bf16[1,1024,1024]{2,1,0:T(8,128)(2,1)} copy(bf16[1,1024,1024]{1,2,0:T(8,128)(2,1)S(1)} %copy-done.4) | data formatting | bytes 4194304
  (66 shorter events, 40.6 us)
Async XLA Ops:
  0.6 18.2 %collective-permute-start.16 = (bf16[2048,128]{1,0:T(8,128)(2,1)}, bf16[2048,128]{1,0:T(8,128)(2,1)S(1)}, u32[]{:S(2)}, u32[]{:S(2)}) collective-permute-start(bf16[2048,128]{1,0:T(8,128)(2,1)} %bitcast.70), channel_id=1, source_target_pairs={{0,1},{1,2},{2,3},{3,4},{4,5},{5,6},{6,7},{7,0},{8,9},{9,10},{10,1... | collective-permute-start | bytes 1572872 | tf_op jit(solution)/shard_map/ppermute | solution.py:77
  18.8 22.1 %collective-permute-start.17 = (bf16[2048,128]{1,0:T(8,128)(2,1)S(1)}, bf16[2048,128]{1,0:T(8,128)(2,1)S(1)}, u32[]{:S(2)}, u32[]{:S(2)}) collective-permute-start(bf16[2048,128]{1,0:T(8,128)(2,1)S(1)} %collective-permute-done.16), channel_id=1, source_target_pairs={{0,1},{1,2},{2,3},{3,4},{4,5},{5,6},{6,7},{7,0},{8,9},{9,10},{10,1... | collective-permute-start | bytes 1572872 | tf_op jit(solution)/shard_map/ppermute | solution.py:77
  18.8 60.0 %collective-permute-start.20 = (bf16[2048,128]{1,0:T(8,128)(2,1)}, bf16[2048,128]{1,0:T(8,128)(2,1)S(1)}, u32[]{:S(2)}, u32[]{:S(2)}) collective-permute-start(bf16[2048,128]{1,0:T(8,128)(2,1)} %bitcast.71), channel_id=1, source_target_pairs={{0,7},{1,0},{2,1},{3,2},{4,3},{5,4},{6,5},{7,6},{8,15},{9,8},{10,9... | collective-permute-start | bytes 1572872 | tf_op jit(solution)/shard_map/ppermute | solution.py:81
  40.9 18.9 %copy-start.6 = (bf16[2048,128]{1,0:T(8,128)(2,1)}, bf16[2048,128]{1,0:T(8,128)(2,1)S(1)}, u32[]{:S(2)}) copy-start(bf16[2048,128]{1,0:T(8,128)(2,1)S(1)} %collective-permute-done.17) | copy-start | bytes 1572868
  40.9 40.1 %collective-permute-start.18 = (bf16[2048,128]{1,0:T(8,128)(2,1)S(1)}, bf16[2048,128]{1,0:T(8,128)(2,1)}, u32[]{:S(2)}, u32[]{:S(2)}) collective-permute-start(bf16[2048,128]{1,0:T(8,128)(2,1)S(1)} %collective-permute-done.17), channel_id=1, source_target_pairs={{0,1},{1,2},{2,3},{3,4},{4,5},{5,6},{6,7},{7,0},{8,9},{9,10},{10,1... | collective-permute-start | bytes 1572872 | tf_op jit(solution)/shard_map/ppermute | solution.py:77
  46.8 5.8 %collective-permute-start = (bf16[1,1024,128]{2,1,0:T(8,128)(2,1)S(1)}, bf16[1,1024,128]{2,1,0:T(8,128)(2,1)S(1)}, u32[]{:S(2)}, u32[]{:S(2)}) collective-permute-start(bf16[1,1024,128]{2,1,0:T(8,128)(2,1)S(1)} %param), channel_id=1, source_target_pairs={{0,8},{8,16},{16,24},{24,0},{1,9},{9,17},{17,25},{25,1},{2,10},{10... | collective-permute-start | bytes 786440 | tf_op jit(solution)/shard_map/cond/branch_0_fun/ppermute | solution.py:19
  52.8 6.0 %collective-permute-start.2 = (bf16[1,1024,128]{2,1,0:T(8,128)(2,1)S(1)}, bf16[1,1024,128]{2,1,0:T(8,128)(2,1)}, u32[]{:S(2)}, u32[]{:S(2)}) collective-permute-start(bf16[1,1024,128]{2,1,0:T(8,128)(2,1)S(1)} %param.2), channel_id=1, source_target_pairs={{0,8},{8,16},{16,24},{24,0},{1,9},{9,17},{17,25},{25,1},{2,10},{10... | collective-permute-start | bytes 786440 | tf_op jit(solution)/shard_map/cond/branch_0_fun/ppermute | solution.py:19
  59.8 6.0 %collective-permute-start.4 = (bf16[1,1024,128]{2,1,0:T(8,128)(2,1)S(1)}, bf16[1,1024,128]{2,1,0:T(8,128)(2,1)}, u32[]{:S(2)}, u32[]{:S(2)}) collective-permute-start(bf16[1,1024,128]{2,1,0:T(8,128)(2,1)S(1)} %param.4), channel_id=1, source_target_pairs={{0,8},{8,16},{16,24},{24,0},{1,9},{9,17},{17,25},{25,1},{2,10},{10... | collective-permute-start | bytes 786440 | tf_op jit(solution)/shard_map/cond/branch_0_fun/ppermute | solution.py:19
  66.9 7.4 %collective-permute-start.7 = (bf16[1,1024,128]{2,1,0:T(8,128)(2,1)}, bf16[1,1024,128]{2,1,0:T(8,128)(2,1)}, u32[]{:S(2)}, u32[]{:S(2)}) collective-permute-start(bf16[1,1024,128]{2,1,0:T(8,128)(2,1)} %param.7), channel_id=1, source_target_pairs={{0,16},{8,24},{16,0},{24,8},{1,17},{9,25},{17,1},{25,9},{2,18},{10... | collective-permute-start | bytes 786440 | tf_op jit(solution)/shard_map/cond/branch_1_fun/ppermute | solution.py:19
  78.8 58.5 %collective-permute-start.21 = (bf16[2048,128]{1,0:T(8,128)(2,1)S(1)}, bf16[2048,128]{1,0:T(8,128)(2,1)}, u32[]{:S(2)}, u32[]{:S(2)}) collective-permute-start(bf16[2048,128]{1,0:T(8,128)(2,1)S(1)} %collective-permute-done.20), channel_id=1, source_target_pairs={{0,7},{1,0},{2,1},{3,2},{4,3},{5,4},{6,5},{7,6},{8,15},{9,8},{10,9... | collective-permute-start | bytes 1572872 | tf_op jit(solution)/shard_map/ppermute | solution.py:81
  81.0 61.0 %collective-permute-start.19 = (bf16[2048,128]{1,0:T(8,128)(2,1)}, bf16[2048,128]{1,0:T(8,128)(2,1)}, u32[]{:S(2)}, u32[]{:S(2)}) collective-permute-start(bf16[2048,128]{1,0:T(8,128)(2,1)} %collective-permute-done.18), channel_id=1, source_target_pairs={{0,1},{1,2},{2,3},{3,4},{4,5},{5,6},{6,7},{7,0},{8,9},{9,10},{10,1... | collective-permute-start | bytes 1572872 | tf_op jit(solution)/shard_map/ppermute | solution.py:77
  82.9 7.9 %copy-start.2 = (bf16[1,1024,1024]{2,1,0:T(8,128)(2,1)S(1)}, bf16[1,1024,1024]{2,1,0:T(8,128)(2,1)}, u32[]{:S(2)}) copy-start(bf16[1,1024,1024]{2,1,0:T(8,128)(2,1)} %param.25) | copy-start | bytes 6291460
  96.3 6.2 %collective-permute-start.8 = (bf16[1,1024,128]{2,1,0:T(8,128)(2,1)}, bf16[1,1024,128]{2,1,0:T(8,128)(2,1)}, u32[]{:S(2)}, u32[]{:S(2)}) collective-permute-start(bf16[1,1024,128]{2,1,0:T(8,128)(2,1)} %param.8), channel_id=1, source_target_pairs={{0,8},{8,16},{16,24},{24,0},{1,9},{9,17},{17,25},{25,1},{2,10},{10... | collective-permute-start | bytes 786440 | tf_op jit(solution)/shard_map/cond/branch_0_fun/ppermute | solution.py:19
  104.4 6.9 %collective-permute-start.11 = (bf16[1,1024,128]{2,1,0:T(8,128)(2,1)}, bf16[1,1024,128]{2,1,0:T(8,128)(2,1)}, u32[]{:S(2)}, u32[]{:S(2)}) collective-permute-start(bf16[1,1024,128]{2,1,0:T(8,128)(2,1)} %param.11), channel_id=1, source_target_pairs={{0,16},{8,24},{16,0},{24,8},{1,17},{9,25},{17,1},{25,9},{2,18},{10... | collective-permute-start | bytes 786440 | tf_op jit(solution)/shard_map/cond/branch_1_fun/ppermute | solution.py:19
  113.1 6.7 %collective-permute-start.13 = (bf16[1,1024,128]{2,1,0:T(8,128)(2,1)}, bf16[1,1024,128]{2,1,0:T(8,128)(2,1)}, u32[]{:S(2)}, u32[]{:S(2)}) collective-permute-start(bf16[1,1024,128]{2,1,0:T(8,128)(2,1)} %param.13), channel_id=1, source_target_pairs={{0,16},{8,24},{16,0},{24,8},{1,17},{9,25},{17,1},{25,9},{2,18},{10... | collective-permute-start | bytes 786440 | tf_op jit(solution)/shard_map/cond/branch_1_fun/ppermute | solution.py:19
  121.7 5.9 %collective-permute-start.14 = (bf16[1,1024,128]{2,1,0:T(8,128)(2,1)S(1)}, bf16[1,1024,128]{2,1,0:T(8,128)(2,1)}, u32[]{:S(2)}, u32[]{:S(2)}) collective-permute-start(bf16[1,1024,128]{2,1,0:T(8,128)(2,1)S(1)} %param.14), channel_id=1, source_target_pairs={{0,8},{8,16},{16,24},{24,0},{1,9},{9,17},{17,25},{25,1},{2,10},{10... | collective-permute-start | bytes 786440 | tf_op jit(solution)/shard_map/cond/branch_0_fun/ppermute | solution.py:19
  129.5 14.9 %copy-start.7 = (bf16[2048,128]{1,0:T(8,128)(2,1)S(1)}, bf16[2048,128]{1,0:T(8,128)(2,1)}, u32[]{:S(2)}) copy-start(bf16[2048,128]{1,0:T(8,128)(2,1)} %copy-done.6) | copy-start | bytes 1572868
  129.5 15.3 %copy-start.5 = (bf16[1,2048,128]{2,1,0:T(8,128)(2,1)S(1)}, bf16[1,2048,128]{2,1,0:T(8,128)(2,1)}, u32[]{:S(2)}) copy-start(bf16[1,2048,128]{2,1,0:T(8,128)(2,1)} %param.23) | copy-start | bytes 1572868
  137.3 15.2 %collective-permute-start.22 = (bf16[2048,128]{1,0:T(8,128)(2,1)}, bf16[2048,128]{1,0:T(8,128)(2,1)S(1)}, u32[]{:S(2)}, u32[]{:S(2)}) collective-permute-start(bf16[2048,128]{1,0:T(8,128)(2,1)} %collective-permute-done.21), channel_id=1, source_target_pairs={{0,7},{1,0},{2,1},{3,2},{4,3},{5,4},{6,5},{7,6},{8,15},{9,8},{10,9... | collective-permute-start | bytes 1572872 | tf_op jit(solution)/shard_map/ppermute | solution.py:81
  152.7 4.8 %copy-start = (f32[1,1024,1024]{2,1,0:T(8,128)S(1)}, f32[1,1024,1024]{2,1,0:T(8,128)}, u32[]{:S(2)}) copy-start(f32[1,1024,1024]{2,1,0:T(8,128)} %param.24) | copy-start | bytes 12582916
  157.5 6.3 %copy-start.1 = (f32[1,1024,1024]{1,2,0:T(8,128)S(1)}, f32[1,1024,1024]{1,2,0:T(8,128)}, u32[]{:S(2)}) copy-start(f32[1,1024,1024]{1,2,0:T(8,128)} %copy.18) | copy-start | bytes 12582916
  157.5 6.3 %copy-start.3 = (bf16[1,1024,1024]{1,2,0:T(8,128)(2,1)S(1)}, bf16[1,1024,1024]{1,2,0:T(8,128)(2,1)}, u32[]{:S(2)}) copy-start(bf16[1,1024,1024]{1,2,0:T(8,128)(2,1)} %copy.19) | copy-start | bytes 6291460
  157.5 6.3 %copy-start.8 = (bf16[1,2048,1024]{2,1,0:T(8,128)(2,1)S(1)}, bf16[1,2048,1024]{2,1,0:T(8,128)(2,1)}, u32[]{:S(2)}) copy-start(bf16[1,2048,1024]{2,1,0:T(8,128)(2,1)} %param.22) | copy-start | bytes 12582916
  180.6 4.1 %copy-start.4 = (bf16[1,1024,1024]{1,2,0:T(8,128)(2,1)S(1)}, bf16[1,1024,1024]{1,2,0:T(8,128)(2,1)}, u32[]{:S(2)}) copy-start(bf16[1,1024,1024]{1,2,0:T(8,128)(2,1)} %get-tuple-element.104) | copy-start | bytes 6291460
